TPU v7x, 512 devices: a whole 4x4x16 slice. The times are simulated.
512 devices in a mesh: gz: 32 (over z, core), gy: 4 (over y), gx: 4 (over x).
Axes of the slice: x: 4, y: 4, z: 16, core: 2. Of those that a mesh axis runs over, the one named last changes fastest.
Arguments:
- pressure: float32 [128, 512, 512], P('gz', 'gy', 'gx'), may hold values from -6 to 6
- light: float32 [4, 3], replicated, may hold values from -4 to 4
- palette: float32 [3, 2], replicated, may hold values from -4 to 4
- rate: float32 [4], replicated, may hold values from 0.00390625 to 0.0234375
- shear: int32 [4, 128, 2], replicated, may hold values from 0 to 8
- offset: int32 [4, 32, 2], replicated, may hold values from 0 to 31
- order: int32 [4, 32], replicated, may hold values from 0 to 31, each once within a row
Outputs:
- picture: float32 [4, 4, 32, 16, 512], P(None, None, 'gz', 'gy', 'gx')
Inputs may be any that keep to these rules, and one draw needn't show every extreme that they name: `order`: each row is a permutation of 0 to 31.
All inputs are finite; a program needn't handle non-finite values.
Results may differ from a plain program's by a relative error of at most 0.00005.
Values sent between devices are 32-bit elements; how exact they have to be, the bound alone decides.
No kernel may reach another device: no remote copies, remote signals or barrier semaphores. Data moves between devices by JAX's collectives and lax.ppermute only.
A program may use at most 64 MiB of HBM per device.

v0:
```python
import jax
import jax.numpy as jnp
from jax import lax
from jax.sharding import PartitionSpec as P

VIEWS = 4
SHEAR = 8
REACH = 32


def padded(cells, sides, width):
    for axis, dim in sides:
        count = lax.axis_size(axis)
        ends = count - 1
        head = lax.slice_in_dim(cells, 0, width, axis=dim)
        tail = lax.slice_in_dim(cells, cells.shape[dim] - width, cells.shape[dim], axis=dim)
        cells = jnp.concatenate(
            [
                lax.ppermute(tail, axis, [(i, (i + 1) % count) for i in range(ends)]),
                cells,
                lax.ppermute(head, axis, [((i + 1) % count, i) for i in range(ends)]),
            ],
            axis=dim,
        )
    return cells


def shifted(value, axis, steps):
    count = lax.axis_size(axis)
    first, last = (max(0, -steps), min(count, count - steps))
    return lax.ppermute(value, axis, [(source, source + steps) for source in range(first, last)])


def surface_terms(slab):
    inner = slab[1:-1, 1:-1, 1:-1]
    grad_depth = 0.5 * (slab[2:, 1:-1, 1:-1] - slab[:-2, 1:-1, 1:-1])
    grad_rows = 0.5 * (slab[1:-1, 2:, 1:-1] - slab[1:-1, :-2, 1:-1])
    grad_cols = 0.5 * (slab[1:-1, 1:-1, 2:] - slab[1:-1, 1:-1, :-2])
    factor = lax.rsqrt(
        grad_depth * grad_depth + grad_rows * grad_rows + grad_cols * grad_cols + 1.0
    )
    return (inner, (grad_depth * factor, grad_rows * factor, grad_cols * factor))


def render_layers(inner, normals, shifts, light, palette, rate, rows, cols):
    lengths = jnp.sqrt(jnp.sum(light * light, axis=1, keepdims=True) + 1.0)
    towards = light / lengths
    offsets = palette[:, 0][:, None, None]
    slopes = palette[:, 1][:, None, None]
    layers = []
    for view in range(light.shape[0]):

        def advance(carry, items):
            color, depth = carry
            value_slab, normal_depth, normal_rows, normal_cols, moved = items
            start = (SHEAR - moved[0], SHEAR - moved[1])
            value = lax.dynamic_slice(value_slab, start, (rows, cols))
            dot = (
                lax.dynamic_slice(normal_depth, start, (rows, cols)) * towards[view, 0]
                + lax.dynamic_slice(normal_rows, start, (rows, cols)) * towards[view, 1]
                + lax.dynamic_slice(normal_cols, start, (rows, cols)) * towards[view, 2]
            )
            shade = 0.25 + 0.75 * dot * dot
            density = rate[view] * (1.0 + jnp.tanh(value))
            alpha = 1.0 - jnp.exp(-density)
            weight = alpha * jnp.exp(-depth)
            hues = jax.nn.sigmoid(offsets + slopes * value[None]) * shade[None]
            return ((color + hues * weight[None], depth + density), None)

        start_carry = (
            jnp.zeros((3, rows, cols), jnp.float32),
            jnp.zeros((rows, cols), jnp.float32),
        )
        (color, depth), _ = lax.scan(
            advance, start_carry, (inner, normals[0], normals[1], normals[2], shifts[view])
        )
        layers.append(jnp.concatenate([color, depth[None]], axis=0))
    return jnp.stack(layers)


def precedence(order):
    bricks = order.shape[1]
    onehot = (order[:, :, None] == jnp.arange(bricks, dtype=jnp.int32)[None, None, :]).astype(
        jnp.float32
    )
    ranks = jnp.sum(onehot * jnp.arange(bricks, dtype=jnp.float32)[None, :, None], axis=1)
    return (ranks[:, None, :] < ranks[:, :, None]).astype(jnp.float32)


def on_device(pressure, light, palette, rate, shear, offset, order):
    depth_cells, rows, cols = pressure.shape
    brick = lax.axis_index("gz")
    zero = jnp.zeros((), jnp.int32)
    widened = padded(pressure, (("gy", 1), ("gx", 2)), SHEAR + 1)
    slab = padded(widened, (("gz", 0),), 1)
    inner, normals = surface_terms(slab)
    shifts = lax.dynamic_slice(shear, (zero, brick * depth_cells, zero), (VIEWS, depth_cells, 2))
    layers = render_layers(inner, normals, shifts, light, palette, rate, rows, cols)
    moved = lax.dynamic_index_in_dim(offset, brick, 1, keepdims=False)
    blank = jnp.zeros((4, rows + REACH, cols + REACH), jnp.float32)
    canvas = jnp.stack(
        [
            lax.dynamic_update_slice(blank, layers[view], (zero, moved[view, 0], moved[view, 1]))
            for view in range(VIEWS)
        ]
    )
    own_tile = canvas[:, :, :rows, :cols]
    from_above = shifted(canvas[:, :, rows:, :cols], "gy", 1)
    from_left = shifted(canvas[:, :, :rows, cols:], "gx", 1)
    from_diagonal = shifted(canvas[:, :, rows:, cols:], ("gy", "gx"), lax.axis_size("gx") + 1)
    from_diagonal = from_diagonal * (lax.axis_index("gx") > 0).astype(jnp.float32)
    own_tile = own_tile.at[:, :, :REACH, :].add(from_above)
    own_tile = own_tile.at[:, :, :, :REACH].add(from_left)
    own_tile = own_tile.at[:, :, :REACH, :REACH].add(from_diagonal)
    ranking = precedence(order)
    pieces = lax.all_to_all(own_tile[None], "gz", split_axis=3, concat_axis=0, tiled=True)
    depths = pieces[:, :, 3]
    cover = jnp.einsum("vbc,cvyx->bvyx", ranking, depths, precision=lax.Precision.HIGHEST)
    colors = jnp.sum(pieces[:, :, :3] * jnp.exp(-cover)[:, :, None], axis=0)
    opacity = 1.0 - jnp.exp(-jnp.sum(depths, axis=0))
    image = jnp.concatenate([colors, opacity[:, None]], axis=1)
    return image[:, :, None]


def solution(mesh):
    return jax.shard_map(
        on_device,
        mesh=mesh,
        in_specs=(P("gz", "gy", "gx"), P(), P(), P(), P(), P(), P()),
        out_specs=P(None, None, "gz", "gy", "gx"),
        check_vma=False,
    )
```

profile of v0, /device:TPU:27, one launch (start us, length us, event | category | flops | bytes accessed | tf_op | source)
XLA Modules:
  0.0 283.3 jit_solution(8438812857838250541)
XLA Ops:
  0.8 2.4 collective-permute-start.1
  9.0 2.2 collective-permute-start.3
  11.2 3.1 %collective-permute-start.2 = (f32[4,146,9]{2,1,0:T(8,128)S(1)}, f32[4,146,9]{2,1,0:T(8,128)S(1)}, u32[]{:S(2)}, u32[]{:S(2)}) collective-permute-start(f32[4,146,9]{2,1,0:T(8,128)S(1)} %get-tuple-element.1120), channel_id=1, source_target_pairs={{0,1},{1,2},{2,3},{4,5},{5,6},{6,7},{8,9},{9,10},{10,11},{12,13},{... | collective-permute-start | bytes 63080 | tf_op jit(solution)/shard_map/ppermute | solution.py:19
  31.5 6.2 %collective-permute-start.5 = (f32[1,146,146]{2,1,0:T(8,128)S(1)}, f32[1,146,146]{2,1,0:T(8,128)S(1)}, u32[]{:S(2)}, u32[]{:S(2)}) collective-permute-start(f32[1,146,146]{2,1,0:T(8,128)S(1)} %get-tuple-element.1118), channel_id=1, source_target_pairs={{0,16},{16,32},{32,48},{48,64},{64,80},{80,96},{96,112},{112,128},... | collective-permute-start | bytes 255800 | tf_op jit(solution)/shard_map/ppermute | solution.py:19
  39.9 4.4 %collective-permute-done.4 = f32[1,146,146]{2,1,0:T(8,128)S(1)} collective-permute-done((f32[1,146,146]{2,1,0:T(8,128)S(1)}, f32[1,146,146]{2,1,0:T(8,128)S(1)}, u32[]{:S(2)}, u32[]{:S(2)}) %collective-permute-start.4) | collective-permute-done | bytes 85296 | tf_op jit(solution)/shard_map/ppermute | solution.py:21
  45.4 2.4 fusion.19
  47.8 31.7 %while.70 = (s32[]{:T(128)}, f32[3,128,128]{2,1,0:T(8,128)S(1)}, f32[128,128]{1,0:T(8,128)S(1)}, f32[3,1,1]{0,2,1:T(1,128)S(1)}, f32[3,1,1]{0,2,1:T(1,128)S(1)},...) while((s32[]{:T(128)}, f32[3,128,128]{2,1,0:T(8,128)S(1)}, ...), condition=%wide.region_8.9_spmd.clone, body=%wide.region_7.8_spmd.clone.sunk | while | flops 753678 | bytes 1442253 | solution.py:74
  53.6 2.0 fusion.65
  61.5 2.0 fusion.65
  69.4 2.0 fusion.65
  77.3 2.0 fusion.65
  79.5 31.0 %while.69 = (s32[]{:T(128)}, f32[3,128,128]{2,1,0:T(8,128)S(1)}, f32[128,128]{1,0:T(8,128)S(1)}, f32[3,1,1]{0,2,1:T(1,128)S(1)}, f32[3,1,1]{0,2,1:T(1,128)S(1)},...) while((s32[]{:T(128)}, f32[3,128,128]{2,1,0:T(8,128)S(1)}, ...), condition=%wide.region_6.7_spmd.clone, body=%wide.region_5.6_spmd.clone.sunk | while | flops 753678 | bytes 1442253 | solution.py:74
  110.5 31.0 %while.68 = (s32[]{:T(128)}, f32[3,128,128]{2,1,0:T(8,128)S(1)}, f32[128,128]{1,0:T(8,128)S(1)}, f32[3,1,1]{0,2,1:T(1,128)S(1)}, f32[3,1,1]{0,2,1:T(1,128)S(1)},...) while((s32[]{:T(128)}, f32[3,128,128]{2,1,0:T(8,128)S(1)}, ...), condition=%wide.region_4.5_spmd.clone, body=%wide.region_3.4_spmd.clone.sunk | while | flops 753678 | bytes 1442253 | solution.py:74
  141.4 24.5 %while.67 = (s32[]{:T(128)}, f32[3,128,128]{2,1,0:T(8,128)S(1)}, f32[128,128]{1,0:T(8,128)S(1)}, f32[3,1,1]{0,2,1:T(1,128)S(1)}, f32[3,1,1]{0,2,1:T(1,128)S(1)},...) while((s32[]{:T(128)}, f32[3,128,128]{2,1,0:T(8,128)S(1)}, ...), condition=%wide.region_2.3_spmd.clone, body=%wide.region_1.2_spmd.clone.sunk | while | flops 753678 | bytes 1442245 | solution.py:74
  166.1 3.1 %dynamic_update_slice.19 = f32[1,4,160,160]{3,2,1,0:T(8,128)S(1)} dynamic-update-slice(f32[1,4,160,160]{3,2,1,0:T(8,128)S(1)} %broadcast_in_dim.30.clone, f32[1,4,128,128]{3,2,1,0:T(8,128)S(1)} %maximum_bitcast_fusion.3, s32[]{:T(128)} %constant.961.clone.1, s32[]{:T(128)} %constant.961.clone.1, s32[]{:T(128)S(6)} %select_n.135, s32[]{:T(128)S(6)} %select_n.136) | dynamic-update-slice | bytes 524292 | tf_op jit(solution)/shard_map/dynamic_update_slice | solution.py:103
  169.3 3.1 %dynamic_update_slice.18 = f32[1,4,160,160]{3,2,1,0:T(8,128)S(1)} dynamic-update-slice(f32[1,4,160,160]{3,2,1,0:T(8,128)S(1)} %broadcast_in_dim.30.clone.1, f32[1,4,128,128]{3,2,1,0:T(8,128)S(1)} %maximum_bitcast_fusion.2, s32[]{:T(128)} %constant.961.clone.1, s32[]{:T(128)} %constant.961.clone.1, s32[]{:T(128)S(6)} %select_n.133, s32[]{:T(128)S(6)} %select_n.134) | dynamic-update-slice | bytes 524292 | tf_op jit(solution)/shard_map/dynamic_update_slice | solution.py:103
  172.5 3.1 %dynamic_update_slice.17 = f32[1,4,160,160]{3,2,1,0:T(8,128)S(1)} dynamic-update-slice(f32[1,4,160,160]{3,2,1,0:T(8,128)S(1)} %broadcast_in_dim.30.clone.2, f32[1,4,128,128]{3,2,1,0:T(8,128)S(1)} %maximum_bitcast_fusion.1, s32[]{:T(128)} %constant.961.clone.1, s32[]{:T(128)} %constant.961.clone.1, s32[]{:T(128)S(6)} %select_n.131, s32[]{:T(128)S(6)} %select_n.132) | dynamic-update-slice | bytes 524292 | tf_op jit(solution)/shard_map/dynamic_update_slice | solution.py:103
  175.7 3.1 %dynamic_update_slice.16 = f32[1,4,160,160]{3,2,1,0:T(8,128)S(1)} dynamic-update-slice(f32[1,4,160,160]{3,2,1,0:T(8,128)S(1)} %broadcast_in_dim.30.clone.3, f32[1,4,128,128]{3,2,1,0:T(8,128)S(1)} %maximum_bitcast_fusion, s32[]{:T(128)} %constant.961.clone.1, s32[]{:T(128)} %constant.961.clone.1, s32[]{:T(128)S(6)} %select_n.129, s32[]{:T(128)S(6)} %select_n.130) | dynamic-update-slice | bytes 524292 | tf_op jit(solution)/shard_map/dynamic_update_slice | solution.py:103
  183.1 3.1 %collective-permute-start.7 = (f32[4,4,128,32]{2,3,1,0:T(8,128)S(1)}, f32[4,4,128,32]{2,3,1,0:T(8,128)S(1)}, u32[]{:S(2)}, u32[]{:S(2)}) collective-permute-start(f32[4,4,128,32]{2,3,1,0:T(8,128)S(1)} %copy.32), channel_id=1, source_target_pairs={{0,1},{1,2},{2,3},{4,5},{5,6},{6,7},{8,9},{9,10},{10,11},{12,13},{... | collective-permute-start | bytes 786440 | tf_op jit(solution)/shard_map/ppermute | solution.py:31
  188.3 2.3 slice.439
  194.2 5.9 %collective-permute-done.6 = f32[4,4,32,128]{3,2,1,0:T(8,128)S(1)} collective-permute-done((f32[4,4,32,128]{3,2,1,0:T(8,128)}, f32[4,4,32,128]{3,2,1,0:T(8,128)S(1)}, u32[]{:S(2)}, u32[]{:S(2)}) %collective-permute-start.6) | collective-permute-done | bytes 262176 | tf_op jit(solution)/shard_map/ppermute | solution.py:31
  202.4 2.0 scatter-add.11
  208.1 17.6 %all-to-all-start = ((f32[1,4,4,128,128]{4,2,1,0,3:T(4,128)}), f32[1,4,4,128,128]{4,2,1,0,3:T(4,128)S(1)}, u32[]{:S(2)}, u32[]{:S(2)}) async-start(f32[1,4,4,128,128]{4,2,1,0,3:T(4,128)} %copy.34), calls=%async_computation | async-start | bytes 2097152 | tf_op jit(solution)/shard_map/all_to_all | solution.py:116
  225.9 55.6 %all-to-all-done = f32[1,4,4,128,128]{4,2,1,0,3:T(4,128)S(1)} async-done(((f32[1,4,4,128,128]{4,2,1,0,3:T(4,128)}), f32[1,4,4,128,128]{4,2,1,0,3:T(4,128)S(1)}, u32[]{:S(2)}, u32[]{:S(2)}) %all-to-all-start) | async-done | bytes 1048608 | tf_op jit(solution)/shard_map/all_to_all | solution.py:116
  (218 shorter events, 100.7 us)
Async XLA Ops:
  0.0 6.8 %copy-start = (s32[4,32,2]{1,2,0:T(2,128)S(1)}, s32[4,32,2]{1,2,0:T(2,128)}, u32[]{:S(2)}) copy-start(s32[4,32,2]{1,2,0:T(2,128)} %param.26) | copy-start | bytes 3076
  0.0 44.3 %copy-start.3 = (f32[4,128,128]{2,1,0:T(8,128)S(1)}, f32[4,128,128]{2,1,0:T(8,128)}, u32[]{:S(2)}) copy-start(f32[4,128,128]{2,1,0:T(8,128)} %param.21) | copy-start | bytes 786436
  0.0 39.6 %copy-start.9 = (s32[4,128,2]{1,2,0:T(2,128)S(1)}, s32[4,128,2]{1,2,0:T(2,128)}, u32[]{:S(2)}) copy-start(s32[4,128,2]{1,2,0:T(2,128)} %param.25) | copy-start | bytes 12292
  0.8 6.2 %collective-permute-start.1 = (f32[4,9,128]{2,1,0:T(8,128)S(1)}, f32[4,9,128]{2,1,0:T(8,128)S(1)}, u32[]{:S(2)}, u32[]{:S(2)}) collective-permute-start(f32[4,9,128]{2,1,0:T(8,128)S(1)} %get-tuple-element.1123), channel_id=1, source_target_pairs={{4,0},{8,4},{12,8},{5,1},{9,5},{13,9},{6,2},{10,6},{14,10},{7,3},{... | collective-permute-start | bytes 55304 | tf_op jit(solution)/shard_map/ppermute | solution.py:21
  3.2 4.7 %collective-permute-start = (f32[4,9,128]{2,1,0:T(8,128)S(1)}, f32[4,9,128]{2,1,0:T(8,128)S(1)}, u32[]{:S(2)}, u32[]{:S(2)}) collective-permute-start(f32[4,9,128]{2,1,0:T(8,128)S(1)} %get-tuple-element.1122), channel_id=1, source_target_pairs={{0,4},{4,8},{8,12},{1,5},{5,9},{9,13},{2,6},{6,10},{10,14},{3,7},{... | collective-permute-start | bytes 55304 | tf_op jit(solution)/shard_map/ppermute | solution.py:19
  9.0 20.9 %collective-permute-start.3 = (f32[4,146,9]{2,1,0:T(8,128)S(1)}, f32[4,146,9]{2,1,0:T(8,128)S(1)}, u32[]{:S(2)}, u32[]{:S(2)}) collective-permute-start(f32[4,146,9]{2,1,0:T(8,128)S(1)} %get-tuple-element.1121), channel_id=1, source_target_pairs={{1,0},{2,1},{3,2},{5,4},{6,5},{7,6},{9,8},{10,9},{11,10},{13,12},{... | collective-permute-start | bytes 63080 | tf_op jit(solution)/shard_map/ppermute | solution.py:21
  11.2 18.8 %collective-permute-start.2 = (f32[4,146,9]{2,1,0:T(8,128)S(1)}, f32[4,146,9]{2,1,0:T(8,128)S(1)}, u32[]{:S(2)}, u32[]{:S(2)}) collective-permute-start(f32[4,146,9]{2,1,0:T(8,128)S(1)} %get-tuple-element.1120), channel_id=1, source_target_pairs={{0,1},{1,2},{2,3},{4,5},{5,6},{6,7},{8,9},{9,10},{10,11},{12,13},{... | collective-permute-start | bytes 63080 | tf_op jit(solution)/shard_map/ppermute | solution.py:19
  29.9 15.4 %copy-start.6 = (f32[4,146,9]{2,1,0:T(8,128)}, f32[4,146,9]{2,1,0:T(8,128)S(1)}, u32[]{:S(2)}) copy-start(f32[4,146,9]{2,1,0:T(8,128)S(1)} %collective-permute-done.3) | copy-start | bytes 63076
  29.9 15.4 %copy-start.7 = (f32[4,146,9]{2,1,0:T(8,128)}, f32[4,146,9]{2,1,0:T(8,128)S(1)}, u32[]{:S(2)}) copy-start(f32[4,146,9]{2,1,0:T(8,128)S(1)} %collective-permute-done.2) | copy-start | bytes 63076
  31.4 14.0 %copy-start.4 = (f32[4,128,128]{2,1,0:T(8,128)S(1)}, f32[4,128,128]{2,1,0:T(8,128)}, u32[]{:S(2)}) copy-start(f32[4,128,128]{2,1,0:T(8,128)} %param.21) | copy-start | bytes 786436
  31.5 8.4 %collective-permute-start.5 = (f32[1,146,146]{2,1,0:T(8,128)S(1)}, f32[1,146,146]{2,1,0:T(8,128)S(1)}, u32[]{:S(2)}, u32[]{:S(2)}) collective-permute-start(f32[1,146,146]{2,1,0:T(8,128)S(1)} %get-tuple-element.1118), channel_id=1, source_target_pairs={{0,16},{16,32},{32,48},{48,64},{64,80},{80,96},{96,112},{112,128},... | collective-permute-start | bytes 255800 | tf_op jit(solution)/shard_map/ppermute | solution.py:19
  37.7 6.5 %collective-permute-start.4 = (f32[1,146,146]{2,1,0:T(8,128)S(1)}, f32[1,146,146]{2,1,0:T(8,128)S(1)}, u32[]{:S(2)}, u32[]{:S(2)}) collective-permute-start(f32[1,146,146]{2,1,0:T(8,128)S(1)} %get-tuple-element.1117), channel_id=1, source_target_pairs={{16,0},{32,16},{48,32},{64,48},{80,64},{96,80},{112,96},{128,112},... | collective-permute-start | bytes 255800 | tf_op jit(solution)/shard_map/ppermute | solution.py:21
  45.4 2.4 copy-start.8
  179.1 1.5 copy-start.2
  183.1 9.7 %collective-permute-start.7 = (f32[4,4,128,32]{2,3,1,0:T(8,128)S(1)}, f32[4,4,128,32]{2,3,1,0:T(8,128)S(1)}, u32[]{:S(2)}, u32[]{:S(2)}) collective-permute-start(f32[4,4,128,32]{2,3,1,0:T(8,128)S(1)} %copy.32), channel_id=1, source_target_pairs={{0,1},{1,2},{2,3},{4,5},{5,6},{6,7},{8,9},{9,10},{10,11},{12,13},{... | collective-permute-start | bytes 786440 | tf_op jit(solution)/shard_map/ppermute | solution.py:31
  187.0 13.1 %collective-permute-start.6 = (f32[4,4,32,128]{3,2,1,0:T(8,128)}, f32[4,4,32,128]{3,2,1,0:T(8,128)S(1)}, u32[]{:S(2)}, u32[]{:S(2)}) collective-permute-start(f32[4,4,32,128]{3,2,1,0:T(8,128)} %pad_maximum_fusion.14), channel_id=1, source_target_pairs={{0,4},{4,8},{8,12},{1,5},{5,9},{9,13},{2,6},{6,10},{10,14},{3,7},{... | collective-permute-start | bytes 786440 | tf_op jit(solution)/shard_map/ppermute | solution.py:31
  191.4 13.1 %collective-permute-start.8 = (f32[4,4,32,32]{3,2,1,0:T(8,128)}, f32[4,4,32,32]{3,2,1,0:T(8,128)}, u32[]{:S(2)}, u32[]{:S(2)}) collective-permute-start(f32[4,4,32,32]{3,2,1,0:T(8,128)} %pad_maximum_fusion.13), channel_id=1, source_target_pairs={{0,5},{1,6},{2,7},{3,8},{4,9},{5,10},{6,11},{7,12},{8,13},{9,14},{... | collective-permute-start | bytes 196616 | tf_op jit(solution)/shard_map/ppermute | solution.py:31
  194.2 6.7 %copy-start.5 = (f32[4,4,128,32]{3,2,1,0:T(8,128)S(1)}, f32[4,4,128,32]{3,2,1,0:T(8,128)}, u32[]{:S(2)}) copy-start(f32[4,4,128,32]{3,2,1,0:T(8,128)} %copy.33) | copy-start | bytes 786436
  200.8 1.5 copy-start.1
  204.4 21.4 %copy-start.10 = (s32[4,32]{1,0:T(4,128)S(1)}, s32[4,32]{1,0:T(4,128)}, u32[]{:S(2)}) copy-start(s32[4,32]{1,0:T(4,128)} %param.27) | copy-start | bytes 1540
  208.1 73.3 %all-to-all-start = ((f32[1,4,4,128,128]{4,2,1,0,3:T(4,128)}), f32[1,4,4,128,128]{4,2,1,0,3:T(4,128)S(1)}, u32[]{:S(2)}, u32[]{:S(2)}) async-start(f32[1,4,4,128,128]{4,2,1,0,3:T(4,128)} %copy.34), calls=%async_computation | async-start | bytes 2097152 | tf_op jit(solution)/shard_map/all_to_all | solution.py:116
where the time goes:
time: 285 us; the launch traced here: 283 us
  waiting for transfers between devices  66.9 us (23%)
  other arithmetic  64.2 us (23%)
  local copies, waits for them, and re-layouts  56.4 us (20%)
  starting transfers between devices  40.6 us (14%)
  loops' own time  39.5 us (14%)
  between operations  15.4 us (5%)
    all_to_all x1, waiting for transfers between devices, on_device(): lax.all_to_all(own_tile[None], 'gz', split_axis=3, concat_axis=0, tiled=T...  55.6 us
    another operation x4, loops' own time, render_layers(): lax.scan(advance, start_carry, (inner, normals[0], normals[1], normals[2]...  39.5 us
    mul x16, other arithmetic, advance(): hues = jax.nn.sigmoid(offsets + slopes * value[None]) * shade[None]  31.1 us
    all_to_all x1, starting transfers between devices, on_device(): lax.all_to_all(own_tile[None], 'gz', split_axis=3, concat_axis=0, tiled=T...  17.6 us
    dynamic_update_slice x4, local copies, waits for them, and re-layouts, on_device(): lax.dynamic_update_slice(blank, layers[view], (zero, moved[view, 0], move...  12.5 us
    add x32, other arithmetic, advance(): return ((color + hues * weight[None], depth + density), None)  11.8 us
    ppermute x3, starting transfers between devices, padded(): lax.ppermute(tail, axis, [(i, (i + 1) % count) for i in range(ends)])  10.6 us
    slice x16, local copies, waits for them, and re-layouts, advance(): towards[view, 0]  9.97 us
  transfers between devices with their start and end apart: 10, of which 5 were waited for; matrix products, arithmetic and copies ran while one was open for 4% of the time, Pallas kernels for 0%

commit v1 on v0

--- a/solution.py
+++ b/solution.py
@@ -113,7 +113,12 @@
     own_tile = own_tile.at[:, :, :, :REACH].add(from_left)
     own_tile = own_tile.at[:, :, :REACH, :REACH].add(from_diagonal)
     ranking = precedence(order)
-    pieces = lax.all_to_all(own_tile[None], "gz", split_axis=3, concat_axis=0, tiled=True)
+    pieces = jnp.concatenate(
+        lax.all_to_all(
+            jnp.stack(jnp.split(own_tile[None], lax.axis_size("gz"), axis=3)), "gz", 0, 0
+        ),
+        axis=0,
+    )
     depths = pieces[:, :, 3]
     cover = jnp.einsum("vbc,cvyx->bvyx", ranking, depths, precision=lax.Precision.HIGHEST)
     colors = jnp.sum(pieces[:, :, :3] * jnp.exp(-cover)[:, :, None], axis=0)

time: 285 us -> 286 us (level)
  no operation moved by 1% of the time
where the time goes in v1:
time: 286 us; the launch traced here: 284 us
  waiting for transfers between devices  66.9 us (23%)
  other arithmetic  64.2 us (22%)
  local copies, waits for them, and re-layouts  56.6 us (20%)
  starting transfers between devices  40.6 us (14%)
  loops' own time  39.5 us (14%)
  between operations  15.5 us (5%)
    all_to_all x1, waiting for transfers between devices, on_device(): lax.all_to_all(jnp.stack(jnp.split(own_tile[None], lax.axis_size('gz'), a...  55.6 us
    another operation x4, loops' own time, render_layers(): lax.scan(advance, start_carry, (inner, normals[0], normals[1], normals[2]...  39.5 us
    mul x16, other arithmetic, advance(): hues = jax.nn.sigmoid(offsets + slopes * value[None]) * shade[None]  31.1 us
    all_to_all x1, starting transfers between devices, on_device(): lax.all_to_all(jnp.stack(jnp.split(own_tile[None], lax.axis_size('gz'), a...  17.6 us
    dynamic_update_slice x4, local copies, waits for them, and re-layouts, on_device(): lax.dynamic_update_slice(blank, layers[view], (zero, moved[view, 0], move...  12.5 us
    add x32, other arithmetic, advance(): return ((color + hues * weight[None], depth + density), None)  11.8 us
    ppermute x3, starting transfers between devices, padded(): lax.ppermute(tail, axis, [(i, (i + 1) % count) for i in range(ends)])  10.6 us
    slice x16, local copies, waits for them, and re-layouts, advance(): towards[view, 0]  9.97 us
  transfers between devices with their start and end apart: 10, of which 5 were waited for; matrix products, arithmetic and copies ran while one was open for 4% of the time, Pallas kernels for 0%

profile of v1, /device:TPU:27, one launch (start us, length us, event | category | flops | bytes accessed | tf_op | source)
XLA Modules:
  0.0 283.6 jit_solution(18301825607352440245)
XLA Ops:
  0.8 2.4 collective-permute-start.1
  9.0 2.2 collective-permute-start.3
  11.2 3.1 %collective-permute-start.2 = (f32[4,146,9]{2,1,0:T(8,128)S(1)}, f32[4,146,9]{2,1,0:T(8,128)S(1)}, u32[]{:S(2)}, u32[]{:S(2)}) collective-permute-start(f32[4,146,9]{2,1,0:T(8,128)S(1)} %get-tuple-element.1120), channel_id=1, source_target_pairs={{0,1},{1,2},{2,3},{4,5},{5,6},{6,7},{8,9},{9,10},{10,11},{12,13},{... | collective-permute-start | bytes 63080 | tf_op jit(solution)/shard_map/ppermute | solution.py:19
  31.5 6.2 %collective-permute-start.5 = (f32[1,146,146]{2,1,0:T(8,128)S(1)}, f32[1,146,146]{2,1,0:T(8,128)S(1)}, u32[]{:S(2)}, u32[]{:S(2)}) collective-permute-start(f32[1,146,146]{2,1,0:T(8,128)S(1)} %get-tuple-element.1118), channel_id=1, source_target_pairs={{0,16},{16,32},{32,48},{48,64},{64,80},{80,96},{96,112},{112,128},... | collective-permute-start | bytes 255800 | tf_op jit(solution)/shard_map/ppermute | solution.py:19
  39.9 4.4 %collective-permute-done.4 = f32[1,146,146]{2,1,0:T(8,128)S(1)} collective-permute-done((f32[1,146,146]{2,1,0:T(8,128)S(1)}, f32[1,146,146]{2,1,0:T(8,128)S(1)}, u32[]{:S(2)}, u32[]{:S(2)}) %collective-permute-start.4) | collective-permute-done | bytes 85296 | tf_op jit(solution)/shard_map/ppermute | solution.py:21
  45.4 2.4 fusion.19
  47.8 31.7 %while.70 = (s32[]{:T(128)}, f32[3,128,128]{2,1,0:T(8,128)S(1)}, f32[128,128]{1,0:T(8,128)S(1)}, f32[3,1,1]{0,2,1:T(1,128)S(1)}, f32[3,1,1]{0,2,1:T(1,128)S(1)},...) while((s32[]{:T(128)}, f32[3,128,128]{2,1,0:T(8,128)S(1)}, ...), condition=%wide.region_8.9_spmd.clone, body=%wide.region_7.8_spmd.clone.sunk | while | flops 753678 | bytes 1442253 | solution.py:74
  53.6 2.0 fusion.65
  61.5 2.0 fusion.65
  69.4 2.0 fusion.65
  77.3 2.0 fusion.65
  79.5 31.0 %while.69 = (s32[]{:T(128)}, f32[3,128,128]{2,1,0:T(8,128)S(1)}, f32[128,128]{1,0:T(8,128)S(1)}, f32[3,1,1]{0,2,1:T(1,128)S(1)}, f32[3,1,1]{0,2,1:T(1,128)S(1)},...) while((s32[]{:T(128)}, f32[3,128,128]{2,1,0:T(8,128)S(1)}, ...), condition=%wide.region_6.7_spmd.clone, body=%wide.region_5.6_spmd.clone.sunk | while | flops 753678 | bytes 1442253 | solution.py:74
  110.5 31.0 %while.68 = (s32[]{:T(128)}, f32[3,128,128]{2,1,0:T(8,128)S(1)}, f32[128,128]{1,0:T(8,128)S(1)}, f32[3,1,1]{0,2,1:T(1,128)S(1)}, f32[3,1,1]{0,2,1:T(1,128)S(1)},...) while((s32[]{:T(128)}, f32[3,128,128]{2,1,0:T(8,128)S(1)}, ...), condition=%wide.region_4.5_spmd.clone, body=%wide.region_3.4_spmd.clone.sunk | while | flops 753678 | bytes 1442253 | solution.py:74
  141.4 24.5 %while.67 = (s32[]{:T(128)}, f32[3,128,128]{2,1,0:T(8,128)S(1)}, f32[128,128]{1,0:T(8,128)S(1)}, f32[3,1,1]{0,2,1:T(1,128)S(1)}, f32[3,1,1]{0,2,1:T(1,128)S(1)},...) while((s32[]{:T(128)}, f32[3,128,128]{2,1,0:T(8,128)S(1)}, ...), condition=%wide.region_2.3_spmd.clone, body=%wide.region_1.2_spmd.clone.sunk | while | flops 753678 | bytes 1442245 | solution.py:74
  166.1 3.1 %dynamic_update_slice.19 = f32[1,4,160,160]{3,2,1,0:T(8,128)S(1)} dynamic-update-slice(f32[1,4,160,160]{3,2,1,0:T(8,128)S(1)} %broadcast_in_dim.30.clone, f32[1,4,128,128]{3,2,1,0:T(8,128)S(1)} %maximum_bitcast_fusion.3, s32[]{:T(128)} %constant.961.clone.1, s32[]{:T(128)} %constant.961.clone.1, s32[]{:T(128)S(6)} %select_n.135, s32[]{:T(128)S(6)} %select_n.136) | dynamic-update-slice | bytes 524292 | tf_op jit(solution)/shard_map/dynamic_update_slice | solution.py:103
  169.3 3.1 %dynamic_update_slice.18 = f32[1,4,160,160]{3,2,1,0:T(8,128)S(1)} dynamic-update-slice(f32[1,4,160,160]{3,2,1,0:T(8,128)S(1)} %broadcast_in_dim.30.clone.1, f32[1,4,128,128]{3,2,1,0:T(8,128)S(1)} %maximum_bitcast_fusion.2, s32[]{:T(128)} %constant.961.clone.1, s32[]{:T(128)} %constant.961.clone.1, s32[]{:T(128)S(6)} %select_n.133, s32[]{:T(128)S(6)} %select_n.134) | dynamic-update-slice | bytes 524292 | tf_op jit(solution)/shard_map/dynamic_update_slice | solution.py:103
  172.5 3.1 %dynamic_update_slice.17 = f32[1,4,160,160]{3,2,1,0:T(8,128)S(1)} dynamic-update-slice(f32[1,4,160,160]{3,2,1,0:T(8,128)S(1)} %broadcast_in_dim.30.clone.2, f32[1,4,128,128]{3,2,1,0:T(8,128)S(1)} %maximum_bitcast_fusion.1, s32[]{:T(128)} %constant.961.clone.1, s32[]{:T(128)} %constant.961.clone.1, s32[]{:T(128)S(6)} %select_n.131, s32[]{:T(128)S(6)} %select_n.132) | dynamic-update-slice | bytes 524292 | tf_op jit(solution)/shard_map/dynamic_update_slice | solution.py:103
  175.7 3.1 %dynamic_update_slice.16 = f32[1,4,160,160]{3,2,1,0:T(8,128)S(1)} dynamic-update-slice(f32[1,4,160,160]{3,2,1,0:T(8,128)S(1)} %broadcast_in_dim.30.clone.3, f32[1,4,128,128]{3,2,1,0:T(8,128)S(1)} %maximum_bitcast_fusion, s32[]{:T(128)} %constant.961.clone.1, s32[]{:T(128)} %constant.961.clone.1, s32[]{:T(128)S(6)} %select_n.129, s32[]{:T(128)S(6)} %select_n.130) | dynamic-update-slice | bytes 524292 | tf_op jit(solution)/shard_map/dynamic_update_slice | solution.py:103
  183.1 3.1 %collective-permute-start.7 = (f32[4,4,128,32]{2,3,1,0:T(8,128)S(1)}, f32[4,4,128,32]{2,3,1,0:T(8,128)S(1)}, u32[]{:S(2)}, u32[]{:S(2)}) collective-permute-start(f32[4,4,128,32]{2,3,1,0:T(8,128)S(1)} %copy.91), channel_id=1, source_target_pairs={{0,1},{1,2},{2,3},{4,5},{5,6},{6,7},{8,9},{9,10},{10,11},{12,13},{... | collective-permute-start | bytes 786440 | tf_op jit(solution)/shard_map/ppermute | solution.py:31
  188.3 2.3 slice.439
  194.2 5.9 %collective-permute-done.6 = f32[4,4,32,128]{3,2,1,0:T(8,128)S(1)} collective-permute-done((f32[4,4,32,128]{3,2,1,0:T(8,128)}, f32[4,4,32,128]{3,2,1,0:T(8,128)S(1)}, u32[]{:S(2)}, u32[]{:S(2)}) %collective-permute-start.6) | collective-permute-done | bytes 262176 | tf_op jit(solution)/shard_map/ppermute | solution.py:31
  202.4 2.0 scatter-add.11
  208.4 17.6 %all-to-all-start = ((f32[32,1,4,4,4,128]{5,4,2,3,1,0:T(4,128)}), f32[32,1,4,4,4,128]{5,4,2,3,1,0:T(4,128)S(1)}, u32[]{:S(2)}, u32[]{:S(2)}) async-start(f32[32,1,4,4,4,128]{5,4,2,3,1,0:T(4,128)} %copy.93), calls=%async_computation | async-start | bytes 2097152 | tf_op jit(solution)/shard_map/all_to_all | solution.py:117
  226.1 55.6 %all-to-all-done = f32[32,1,4,4,4,128]{5,4,2,3,1,0:T(4,128)S(1)} async-done(((f32[32,1,4,4,4,128]{5,4,2,3,1,0:T(4,128)}), f32[32,1,4,4,4,128]{5,4,2,3,1,0:T(4,128)S(1)}, u32[]{:S(2)}, u32[]{:S(2)}) %all-to-all-start) | async-done | bytes 1048608 | tf_op jit(solution)/shard_map/all_to_all | solution.py:117
  (250 shorter events, 100.9 us)
Async XLA Ops:
  0.0 6.8 %copy-start = (s32[4,32,2]{1,2,0:T(2,128)S(1)}, s32[4,32,2]{1,2,0:T(2,128)}, u32[]{:S(2)}) copy-start(s32[4,32,2]{1,2,0:T(2,128)} %param.26) | copy-start | bytes 3076
  0.0 44.3 %copy-start.3 = (f32[4,128,128]{2,1,0:T(8,128)S(1)}, f32[4,128,128]{2,1,0:T(8,128)}, u32[]{:S(2)}) copy-start(f32[4,128,128]{2,1,0:T(8,128)} %param.21) | copy-start | bytes 786436
  0.0 39.6 %copy-start.9 = (s32[4,128,2]{1,2,0:T(2,128)S(1)}, s32[4,128,2]{1,2,0:T(2,128)}, u32[]{:S(2)}) copy-start(s32[4,128,2]{1,2,0:T(2,128)} %param.25) | copy-start | bytes 12292
  0.8 6.2 %collective-permute-start.1 = (f32[4,9,128]{2,1,0:T(8,128)S(1)}, f32[4,9,128]{2,1,0:T(8,128)S(1)}, u32[]{:S(2)}, u32[]{:S(2)}) collective-permute-start(f32[4,9,128]{2,1,0:T(8,128)S(1)} %get-tuple-element.1123), channel_id=1, source_target_pairs={{4,0},{8,4},{12,8},{5,1},{9,5},{13,9},{6,2},{10,6},{14,10},{7,3},{... | collective-permute-start | bytes 55304 | tf_op jit(solution)/shard_map/ppermute | solution.py:21
  3.2 4.7 %collective-permute-start = (f32[4,9,128]{2,1,0:T(8,128)S(1)}, f32[4,9,128]{2,1,0:T(8,128)S(1)}, u32[]{:S(2)}, u32[]{:S(2)}) collective-permute-start(f32[4,9,128]{2,1,0:T(8,128)S(1)} %get-tuple-element.1122), channel_id=1, source_target_pairs={{0,4},{4,8},{8,12},{1,5},{5,9},{9,13},{2,6},{6,10},{10,14},{3,7},{... | collective-permute-start | bytes 55304 | tf_op jit(solution)/shard_map/ppermute | solution.py:19
  9.0 20.9 %collective-permute-start.3 = (f32[4,146,9]{2,1,0:T(8,128)S(1)}, f32[4,146,9]{2,1,0:T(8,128)S(1)}, u32[]{:S(2)}, u32[]{:S(2)}) collective-permute-start(f32[4,146,9]{2,1,0:T(8,128)S(1)} %get-tuple-element.1121), channel_id=1, source_target_pairs={{1,0},{2,1},{3,2},{5,4},{6,5},{7,6},{9,8},{10,9},{11,10},{13,12},{... | collective-permute-start | bytes 63080 | tf_op jit(solution)/shard_map/ppermute | solution.py:21
  11.2 18.8 %collective-permute-start.2 = (f32[4,146,9]{2,1,0:T(8,128)S(1)}, f32[4,146,9]{2,1,0:T(8,128)S(1)}, u32[]{:S(2)}, u32[]{:S(2)}) collective-permute-start(f32[4,146,9]{2,1,0:T(8,128)S(1)} %get-tuple-element.1120), channel_id=1, source_target_pairs={{0,1},{1,2},{2,3},{4,5},{5,6},{6,7},{8,9},{9,10},{10,11},{12,13},{... | collective-permute-start | bytes 63080 | tf_op jit(solution)/shard_map/ppermute | solution.py:19
  29.9 15.4 %copy-start.6 = (f32[4,146,9]{2,1,0:T(8,128)}, f32[4,146,9]{2,1,0:T(8,128)S(1)}, u32[]{:S(2)}) copy-start(f32[4,146,9]{2,1,0:T(8,128)S(1)} %collective-permute-done.3) | copy-start | bytes 63076
  29.9 15.4 %copy-start.7 = (f32[4,146,9]{2,1,0:T(8,128)}, f32[4,146,9]{2,1,0:T(8,128)S(1)}, u32[]{:S(2)}) copy-start(f32[4,146,9]{2,1,0:T(8,128)S(1)} %collective-permute-done.2) | copy-start | bytes 63076
  31.4 14.0 %copy-start.4 = (f32[4,128,128]{2,1,0:T(8,128)S(1)}, f32[4,128,128]{2,1,0:T(8,128)}, u32[]{:S(2)}) copy-start(f32[4,128,128]{2,1,0:T(8,128)} %param.21) | copy-start | bytes 786436
  31.5 8.4 %collective-permute-start.5 = (f32[1,146,146]{2,1,0:T(8,128)S(1)}, f32[1,146,146]{2,1,0:T(8,128)S(1)}, u32[]{:S(2)}, u32[]{:S(2)}) collective-permute-start(f32[1,146,146]{2,1,0:T(8,128)S(1)} %get-tuple-element.1118), channel_id=1, source_target_pairs={{0,16},{16,32},{32,48},{48,64},{64,80},{80,96},{96,112},{112,128},... | collective-permute-start | bytes 255800 | tf_op jit(solution)/shard_map/ppermute | solution.py:19
  37.7 6.5 %collective-permute-start.4 = (f32[1,146,146]{2,1,0:T(8,128)S(1)}, f32[1,146,146]{2,1,0:T(8,128)S(1)}, u32[]{:S(2)}, u32[]{:S(2)}) collective-permute-start(f32[1,146,146]{2,1,0:T(8,128)S(1)} %get-tuple-element.1117), channel_id=1, source_target_pairs={{16,0},{32,16},{48,32},{64,48},{80,64},{96,80},{112,96},{128,112},... | collective-permute-start | bytes 255800 | tf_op jit(solution)/shard_map/ppermute | solution.py:21
  45.4 2.4 copy-start.8
  179.1 1.5 copy-start.2
  183.1 9.7 %collective-permute-start.7 = (f32[4,4,128,32]{2,3,1,0:T(8,128)S(1)}, f32[4,4,128,32]{2,3,1,0:T(8,128)S(1)}, u32[]{:S(2)}, u32[]{:S(2)}) collective-permute-start(f32[4,4,128,32]{2,3,1,0:T(8,128)S(1)} %copy.91), channel_id=1, source_target_pairs={{0,1},{1,2},{2,3},{4,5},{5,6},{6,7},{8,9},{9,10},{10,11},{12,13},{... | collective-permute-start | bytes 786440 | tf_op jit(solution)/shard_map/ppermute | solution.py:31
  187.0 13.1 %collective-permute-start.6 = (f32[4,4,32,128]{3,2,1,0:T(8,128)}, f32[4,4,32,128]{3,2,1,0:T(8,128)S(1)}, u32[]{:S(2)}, u32[]{:S(2)}) collective-permute-start(f32[4,4,32,128]{3,2,1,0:T(8,128)} %pad_maximum_fusion.14), channel_id=1, source_target_pairs={{0,4},{4,8},{8,12},{1,5},{5,9},{9,13},{2,6},{6,10},{10,14},{3,7},{... | collective-permute-start | bytes 786440 | tf_op jit(solution)/shard_map/ppermute | solution.py:31
  191.3 13.0 %collective-permute-start.8 = (f32[4,4,32,32]{3,2,1,0:T(8,128)}, f32[4,4,32,32]{3,2,1,0:T(8,128)}, u32[]{:S(2)}, u32[]{:S(2)}) collective-permute-start(f32[4,4,32,32]{3,2,1,0:T(8,128)} %pad_maximum_fusion.13), channel_id=1, source_target_pairs={{0,5},{1,6},{2,7},{3,8},{4,9},{5,10},{6,11},{7,12},{8,13},{9,14},{... | collective-permute-start | bytes 196616 | tf_op jit(solution)/shard_map/ppermute | solution.py:31
  194.2 6.7 %copy-start.5 = (f32[4,4,128,32]{3,2,1,0:T(8,128)S(1)}, f32[4,4,128,32]{3,2,1,0:T(8,128)}, u32[]{:S(2)}) copy-start(f32[4,4,128,32]{3,2,1,0:T(8,128)} %copy.92) | copy-start | bytes 786436
  200.8 1.5 copy-start.1
  206.8 19.2 %copy-start.10 = (s32[4,32]{1,0:T(4,128)S(1)}, s32[4,32]{1,0:T(4,128)}, u32[]{:S(2)}) copy-start(s32[4,32]{1,0:T(4,128)} %param.27) | copy-start | bytes 1540
  208.4 73.3 %all-to-all-start = ((f32[32,1,4,4,4,128]{5,4,2,3,1,0:T(4,128)}), f32[32,1,4,4,4,128]{5,4,2,3,1,0:T(4,128)S(1)}, u32[]{:S(2)}, u32[]{:S(2)}) async-start(f32[32,1,4,4,4,128]{5,4,2,3,1,0:T(4,128)} %copy.93), calls=%async_computation | async-start | bytes 2097152 | tf_op jit(solution)/shard_map/all_to_all | solution.py:117
